TPU v7x, 256 devices: a whole 4x4x8 slice. The times are simulated.
256 devices in a mesh: example: 32 (over z_hi, x, core), tensor: 8 (over z_lo, y).
Axes of the slice: x: 4, y: 4, z: 8 (z_hi: 4, z_lo: 2; z = z_hi * 2 + z_lo), core: 2. Of those that a mesh axis runs over, the one named last changes fastest.
Arguments:
- layer_input: bfloat16 [16384, 4096], P('example', 'tensor'), may hold values from -6 to 6
- gate_act: bfloat16 [16384, 14336], P('example', 'tensor'), may hold values from -8 to 8
- hidden_grad: bfloat16 [16384, 14336], P('example', 'tensor'), may hold values from -6 to 6
- up_weight: bfloat16 [4096, 14336], P('example', 'tensor'), may hold values from -0.046875 to 0.046875
- proj_input: bfloat16 [4096, 64], P('tensor'), may hold values from -0.09375 to 0.09375
- proj_output: bfloat16 [14336, 64], P('tensor'), may hold values from -0.046875 to 0.046875
- sequence_ids: int32 [16384], P('example'), may hold values from 0 to 127, as said below
Outputs:
- input_grad: bfloat16 [16384, 4096], P('example', 'tensor')
- features: float32 [128, 4096], P('example')
- hessian: float32 [4096, 4096], P('example', 'tensor')
Inputs may be any that keep to these rules, and one draw needn't show every extreme that they name: `sequence_ids`: token block b (tokens b * 512 to (b + 1) * 512 - 1) holds exactly the 4 examples b * 4 to (b + 1) * 4 - 1, each a run of one or more tokens, in order; the first token of a block starts its first example.
All inputs are finite; a program needn't handle non-finite values.
Results may differ from a plain program's by a relative error of at most 0.0049.
Values may be sent and summed in bfloat16 or wider, within the bound.
A program may use at most 128 MiB of HBM per device.

v0:
```python
import jax
import jax.numpy as jnp
from jax import lax
from jax.sharding import PartitionSpec as P

SEQS_DEV = 4


damping = 0.1


def example_grads(onehot, input_low, output_low):
    count_rows = input_low.shape[0]
    rank_size = input_low.shape[1]
    weighted = (onehot[:, :, None] * input_low[:, None, :]).reshape(
        count_rows, onehot.shape[1] * rank_size
    )
    grads = jnp.dot(
        weighted.T, output_low, precision=lax.Precision.HIGHEST, preferred_element_type=jnp.float32
    )
    return grads.reshape(onehot.shape[1], rank_size * output_low.shape[1])


def body(layer_input, gate_act, hidden_grad, up_weight, proj_input, proj_output, sequence_ids):
    up_grad = (hidden_grad.astype(jnp.float32) * jax.nn.silu(gate_act.astype(jnp.float32))).astype(
        jnp.bfloat16
    )
    input_part = jnp.dot(layer_input, proj_input, preferred_element_type=jnp.float32)
    output_part = jnp.dot(up_grad, proj_output, preferred_element_type=jnp.float32)
    token_count = layer_input.shape[0]
    local_ids = sequence_ids - sequence_ids[0]
    onehot = (local_ids[:, None] == jnp.arange(SEQS_DEV, dtype=jnp.int32)[None, :]).astype(
        jnp.float32
    )
    factor = (SEQS_DEV / token_count) ** 0.5
    input_low, output_low = lax.psum((input_part, output_part), "tensor")
    features = example_grads(onehot, input_low, output_low) * factor
    partial_terms = lax.dot_general(
        up_grad,
        lax.all_gather(up_weight, "example", axis=0, tiled=True),
        (((1,), (1,)), ((), ())),
        preferred_element_type=jnp.float32,
    )
    input_grad = lax.psum_scatter(partial_terms, "tensor", scatter_dimension=1, tiled=True).astype(
        jnp.bfloat16
    )
    feat_size = features.shape[1]
    row_width = feat_size // lax.axis_size("example")
    col_width = feat_size // lax.axis_size("tensor")
    ex_index = lax.axis_index("example")
    tp_index = lax.axis_index("tensor")
    gathered = lax.all_gather(features, "example", axis=0, tiled=True)
    row_block = lax.dynamic_slice_in_dim(gathered, ex_index * row_width, row_width, 1)
    col_block = lax.dynamic_slice_in_dim(gathered, tp_index * col_width, col_width, 1)
    gram_tile = lax.dot_general(
        row_block,
        col_block,
        (((0,), (0,)), ((), ())),
        precision=lax.Precision.HIGHEST,
        preferred_element_type=jnp.float32,
    )
    gram_tile = gram_tile / row_block.shape[0]
    row_global = ex_index * row_width + jnp.arange(row_width, dtype=jnp.int32)[:, None]
    col_global = tp_index * col_width + jnp.arange(col_width, dtype=jnp.int32)[None, :]
    hessian = gram_tile + damping * (row_global == col_global).astype(jnp.float32)
    return (input_grad, features, hessian)


def solution(mesh):
    return jax.shard_map(
        body,
        mesh=mesh,
        in_specs=(
            P("example", "tensor"),
            P("example", "tensor"),
            P("example", "tensor"),
            P("example", "tensor"),
            P("tensor", None),
            P("tensor", None),
            P("example"),
        ),
        out_specs=(P("example", "tensor"), P("example", None), P("example", "tensor")),
        check_vma=False,
    )
```

profile of v0, /device:TPU:1, one launch (start us, length us, event | category | flops | bytes accessed | tf_op | source)
XLA Modules:
  0.0 272.4 jit_solution(16151407130093382255)
XLA Ops:
  8.0 0.0 copy-start
  8.0 0.0 copy-start.2
  8.0 0.0 copy-start.1
  8.0 0.0 all-reduce.3.cloned.1.call-start
  8.1 3.2 %fusion.4 = bf16[512,1792]{1,0:T(8,128)(2,1)S(1)} fusion(bf16[512,1792]{1,0:T(8,128)(2,1)} %param.8, bf16[512,1792]{1,0:T(8,128)(2,1)} %param.9), kind=kLoop, calls=%fused_computation.6 | loop fusion | flops 7340032 | bytes 5505024 | tf_op jit(solution)/shard_map/convert_element_type | solution.py:25
  11.3 0.0 copy-done
  11.3 0.0 copy-done.2
  11.3 0.0 copy-start.3
  11.4 0.9 fusion.11
  12.3 1.3 fusion.12
  13.6 0.0 all-reduce.3.cloned.1.call-update
  13.7 0.0 all-gather.4.cloned.1.call-start
  13.7 0.5 all-gather.4.cloned.1.call-update
  14.2 0.0 all-gather.6.cloned.1.call-start
  14.3 0.5 slice.3
  14.8 0.6 broadcast_subtract_fusion
  15.5 121.1 %all-reduce.3.cloned.1.call-done = (f32[512,64]{0,1:T(8,128)}, f32[512,64]{0,1:T(8,128)}) async-done(((f32[512,64]{0,1:T(8,128)}, f32[512,64]{0,1:T(8,128)}), (f32[512,64]{0,1:T(8,128)}, f32[512,64]{0,1:T(8,128)})) %all-reduce.3.cloned.1.call-update) | async-done | bytes 262160 | tf_op jit(solution)/shard_map/psum | solution.py:36
  136.5 1.0 broadcast_multiply_fusion
  137.5 1.5 convolution_multiply_fusion.1
  139.0 0.1 copy.13
  139.1 0.7 reshape.46
  139.8 0.0 all-gather.6.cloned.1.call-update
  139.9 0.0 reduce-scatter.2.cloned.1.call-start
  139.9 0.0 all-gather.4.cloned.1.call-done
  139.9 13.1 %fusion.10 = f32[512,4096]{1,0:T(8,128)} fusion(bf16[512,1792]{1,0:T(8,128)(2,1)S(1)} %fusion.4, bf16[4096,1792]{1,0:T(8,128)(2,1)} %all-gather.4.cloned.1.call-done), kind=kOutput, calls=%fused_computation.19 | convolution fusion | flops 7516192768 | bytes 24903680 | tf_op jit(solution)/shard_map/dot_general | solution.py:38
  153.1 0.0 reduce-scatter.2.cloned.1.call-update
  153.1 0.7 mul.55
  153.9 67.9 %all-gather.6.cloned.1.call-done = f32[32,4,4096]{2,1,0:T(4,128)} async-done(((f32[1,4,4096]{2,1,0:T(4,128)}), f32[32,4,4096]{2,1,0:T(4,128)}) %all-gather.6.cloned.1.call-update) | async-done | bytes 2097168 | tf_op jit(solution)/shard_map/all_gather | solution.py:52
  221.7 2.0 reshape.47
  223.7 1.1 fusion.5
  224.9 38.0 %reduce-scatter.2.cloned.1.call-done = f32[512,512]{1,0:T(8,128)} async-done(((f32[512,4096]{1,0:T(8,128)}), f32[512,512]{1,0:T(8,128)}) %reduce-scatter.2.cloned.1.call-update) | async-done | bytes 1048592 | tf_op jit(solution)/shard_map/reduce_scatter | solution.py:44
  262.9 2.1 convert_element_type.23
  (5 shorter events, 0.0 us)
Async XLA Ops:
  8.0 3.3 %copy-start = (bf16[512,512]{1,0:T(8,128)(2,1)S(1)}, bf16[512,512]{1,0:T(8,128)(2,1)}, u32[]{:S(2)}) copy-start(bf16[512,512]{1,0:T(8,128)(2,1)} %param.7) | copy-start | bytes 1572868
  8.0 3.3 %copy-start.2 = (bf16[512,64]{0,1:T(8,128)(2,1)S(1)}, bf16[512,64]{0,1:T(8,128)(2,1)}, u32[]{:S(2)}) copy-start(bf16[512,64]{0,1:T(8,128)(2,1)} %param.11) | copy-start | bytes 196612
  8.0 4.3 %copy-start.1 = (bf16[1792,64]{0,1:T(8,128)(2,1)S(1)}, bf16[1792,64]{0,1:T(8,128)(2,1)}, u32[]{:S(2)}) copy-start(bf16[1792,64]{0,1:T(8,128)(2,1)} %param.12) | copy-start | bytes 688132
  8.0 128.5 %all-reduce.3.cloned.1.call-start = ((), (), s32[]{:S(2)}) async-start(), calls=%async_computation.4 | async-start | bytes 524288 | tf_op jit(solution)/shard_map/psum | solution.py:36
  11.3 2.9 %copy-start.3 = (s32[512]{0:T(512)S(1)}, s32[512]{0:T(512)}, u32[]{:S(2)}) copy-start(s32[512]{0:T(512)} %param.13) | copy-start | bytes 6148
  13.7 126.3 %all-gather.4.cloned.1.call-start = ((), (), s32[]{:S(2)}) async-start(), calls=%async_computation.1 | async-start | bytes 15138816 | tf_op jit(solution)/shard_map/all_gather | solution.py:40
  14.2 207.5 %all-gather.6.cloned.1.call-start = ((), (), s32[]{:S(2)}) async-start(), calls=%async_computation.3 | async-start | bytes 2162688 | tf_op jit(solution)/shard_map/all_gather | solution.py:52
  139.9 123.0 %reduce-scatter.2.cloned.1.call-start = ((), (), s32[]{:S(2)}) async-start(), calls=%async_computation.2 | async-start | bytes 9437184 | tf_op jit(solution)/shard_map/reduce_scatter | solution.py:44
Sparse Core Ops, SparseCore 0:
  13.8 122.7 all-reduce.2
  153.2 109.6 reduce-scatter.1
Sparse Core Ops, SparseCore 1:
  17.0 114.0 all-gather.3
  139.9 81.7 all-gather.5
where the time goes:
time: 273 us; the launch traced here: 272 us
  waiting for transfers between devices  228 us (84%)
  matrix products  18 us (7%)
  between operations  15.6 us (6%)
  other arithmetic  6.94 us (3%)
  local copies, waits for them, and re-layouts  4.11 us (2%)
    psum x1, waiting for transfers between devices, body(): input_low, output_low = lax.psum((input_part, output_part), 'tensor')  121 us
    all_gather x1, waiting for transfers between devices, body(): gathered = lax.all_gather(features, 'example', axis=0, tiled=True)  67.9 us
    reduce_scatter x1, waiting for transfers between devices, body(): lax.psum_scatter(partial_terms, 'tensor', scatter_dimension=1, tiled=True)  38 us
    dot_general x1, matrix products, body(): lax.dot_general(up_grad, lax.all_gather(up_weight, 'example', axis=0, til...  13.1 us
  transfers between devices with their start and end apart: 4, of which 3 were waited for; matrix products, arithmetic and copies ran while one was open for 8% of the time, Pallas kernels for 0%

commit v1 on v0

v1 whole, which is shorter than its diff:
```python
import jax
import jax.numpy as jnp
from jax import lax
from jax.experimental import pallas as pl
from jax.experimental.pallas import tpu as pltpu
from jax.sharding import PartitionSpec as P

MESH = pl.DeviceIdType.MESH
F32 = jnp.float32
BF16 = jnp.bfloat16
HIGHEST = lax.Precision.HIGHEST

DAMPING = 0.1
TOK = 512
KDIM = 1792
RANK = 64
ROUNDS = 4
ROWS = 32
PAIR_TILES = [[(i, a) for a in range(i + 1)] + [(r, i) for r in range(i)] for i in range(ROUNDS)]
NT = [4 + len(PAIR_TILES[i]) for i in range(ROUNDS)]


class Copies:
    def __init__(self, send_sems, recv_sems):
        self.send, self.recv, self.count, self.sent = send_sems, recv_sems, 0, []

    def make(self, src, dst, device):
        index = self.count
        self.count += 1
        copy = pltpu.make_async_remote_copy(
            src_ref=src,
            dst_ref=dst,
            send_sem=self.send.at[index],
            recv_sem=self.recv.at[index],
            device_id=device,
            device_id_type=MESH,
        )
        return copy

    def go(self, src, dst, device):
        copy = self.make(src, dst, device)
        copy.start()
        self.sent.append(copy)
        return copy


N_COPIES = 192


def kernel(
    x_in, gate_in, hid_in, w_in, pi_in, po_in, ids_ref,
    o_ref, feat_ref, hess_ref,
    xv, gv, hv, piv, pov, a_own, a_pair, wbuf,
    sb0, sb1, sb2, sb3, r1p, r1m, r2m, r2p, zs, zr, sown, xs, xr,
    low, lowr, fpart, fpr, fmine, fsib, gcol, rowb,
    send_sems, recv_sems, loc_sems,
):
    e = lax.axis_index("example")
    t = lax.axis_index("tensor")
    zh, x, c = e // 8, (e // 2) % 4, e % 2
    zl, y = t // 4, t % 4

    def ex(zh_, x_, c_):
        return zh_ * 8 + x_ * 2 + c_

    def te(zl_, y_):
        return zl_ * 4 + y_

    sib = (ex(zh, x, 1 - c), t)
    pair = (ex(zh, x + 1 - 2 * (x % 2), c), t)
    qdev = (ex(zh, 3 - x, c), t)
    zp = (ex((zh + 1) % 4, x, c), t)
    zm = (ex((zh + 3) % 4, x, c), t)
    yp = (e, te(zl, (y + 1) % 4))
    ym = (e, te(zl, (y + 3) % 4))
    zlp = (e, te(1 - zl, y))
    xs_dev = {dx: (ex(zh, (x + dx) % 4, c), t) for dx in (1, 2, 3)}
    zs_dev = {dz: (ex((zh + dz) % 4, x, c), t) for dz in (1, 2, 3)}
    tens = [(dzl, dy) for dzl in range(2) for dy in range(4) if (dzl, dy) != (0, 0)]
    tidx = {d: te((zl + d[0]) % 2, (y + d[1]) % 4) for d in tens}

    barrier = pltpu.get_barrier_semaphore()
    partners = [sib] + list(xs_dev.values()) + list(zs_dev.values()) + [(e, tidx[d]) for d in tens]
    for dev in partners:
        pl.semaphore_signal(barrier, inc=1, device_id=dev, device_id_type=MESH)

    loads = []

    def load(src, dst):
        copy = pltpu.make_async_copy(src, dst, loc_sems.at[len(loads)])
        copy.start()
        loads.append(copy)
        return copy

    w_load = [load(w_in.at[pl.ds(r * ROWS, ROWS)], wbuf.at[r, 0, c]) for r in range(ROUNDS)]
    gh_load = []
    for a in range(4):
        rows = pl.ds(a * 128, 128)
        gh_load.append((load(gate_in.at[rows], gv.at[rows]), load(hid_in.at[rows], hv.at[rows])))
    low_load = [load(x_in, xv), load(pi_in, piv), load(po_in, pov)]

    pl.semaphore_wait(barrier, len(partners))
    cp = Copies(send_sems, recv_sems)

    def slot(r, dz, s, core):
        return wbuf.at[r, (dz % 2) * 2 + s, (dz // 2) * 2 + core]

    w_z = {}
    w_x = {}
    w_s = {}

    def own_sends(r):
        w_load[r].wait()
        w_z[r, 3] = cp.go(slot(r, 0, 0, c), slot(r, 3, 0, c), zp)
        w_z[r, 1] = cp.go(slot(r, 0, 0, c), slot(r, 1, 0, c), zm)
        w_x[r, 0] = cp.go(slot(r, 0, 0, c), slot(r, 0, 1, c), qdev)
        w_s[r, 0, 0] = cp.go(slot(r, 0, 0, c), slot(r, 0, 0, c), sib)

    def s1(r):
        w_z[r, 3].wait_recv()
        half = pl.ds(0, ROWS // 2)
        w_z[r, "2a"] = cp.go(slot(r, 3, 0, c).at[half], slot(r, 2, 0, c).at[half], zp)
        w_x[r, 3] = cp.go(slot(r, 3, 0, c), slot(r, 3, 1, c), qdev)
        w_s[r, 3, 0] = cp.go(slot(r, 3, 0, c), slot(r, 3, 0, c), sib)
        w_z[r, 1].wait_recv()
        half = pl.ds(ROWS // 2, ROWS // 2)
        w_z[r, "2b"] = cp.go(slot(r, 1, 0, c).at[half], slot(r, 2, 0, c).at[half], zm)
        w_x[r, 1] = cp.go(slot(r, 1, 0, c), slot(r, 1, 1, c), qdev)
        w_s[r, 1, 0] = cp.go(slot(r, 1, 0, c), slot(r, 1, 0, c), sib)
        if r + 2 < ROUNDS:
            own_sends(r + 2)

    def s2(r):
        w_z[r, "2a"].wait_recv()
        w_z[r, "2b"].wait_recv()
        w_x[r, 2] = cp.go(slot(r, 2, 0, c), slot(r, 2, 1, c), qdev)
        w_s[r, 2, 0] = cp.go(slot(r, 2, 0, c), slot(r, 2, 0, c), sib)

    def s3(r):
        for dz in (0, 3, 1, 2):
            w_x[r, dz].wait_recv()
            w_s[r, dz, 1] = cp.go(slot(r, dz, 1, c), slot(r, dz, 1, c), sib)

    def s4(r):
        for dz in (0, 3, 1, 2):
            for s in range(2):
                w_s[r, dz, s].wait_recv()

    own_sends(0)
    own_sends(1)

    a_copy = []
    for a in range(4):
        for copy in gh_load[a]:
            copy.wait()

        def up(j, _, a=a):
            rows = pl.ds(a * 128 + j * 16, 16)
            g = gv[rows].astype(F32)
            h = hv[rows].astype(F32)
            a_own[rows] = (h * (g / (1.0 + jnp.exp(-g)))).astype(BF16)
            return 0

        lax.fori_loop(0, 8, up, 0)
        rows = pl.ds(a * 128, 128)
        a_copy.append(cp.go(a_own.at[rows], a_pair.at[rows], pair))

    for copy in low_load:
        copy.wait()
    for n in range(4):
        rows = pl.ds(n * 128, 128)
        one = jnp.dot(xv[rows], piv[...], preferred_element_type=F32)
        two = jnp.dot(a_own[rows], pov[...], preferred_element_type=F32)
        both = jnp.concatenate([one, two], axis=1)
        low[2 * n] = both[:64]
        low[2 * n + 1] = both[64:]
    l2 = [cp.go(low.at[tidx[d]], lowr.at[i], (e, tidx[d])) for i, d in enumerate(tens)]
    lc = {}

    def l3():
        total = low[t]
        for i in range(7):
            l2[i].wait_recv()
            total = total + lowr[i]
        lane = lax.broadcasted_iota(jnp.int32, (64, 128), 1)
        out2 = jnp.where(lane < 64, pltpu.roll(total, 64, 1), total)
        out8 = jnp.concatenate([out2] * 4, axis=1)
        local = ids_ref[pl.ds(t, 1), :] - 4 * e + 4 * c
        hot = (lax.broadcasted_iota(jnp.int32, (8, 64), 0) == local).astype(F32)
        hot = hot * ((4 / 512) ** 0.5)

        def piece(j, _):
            spread = (
                lax.broadcasted_iota(jnp.int32, (128, 512), 0)
                == lax.broadcasted_iota(jnp.int32, (128, 512), 1) // 64 + 8 * j
            ).astype(F32)
            rep = jnp.dot(total, spread, precision=HIGHEST, preferred_element_type=F32)
            fpart[j] = jnp.dot(hot, rep * out8, precision=HIGHEST, preferred_element_type=F32)
            return 0

        lax.fori_loop(0, 8, piece, 0)
        lc["f"] = [cp.go(fpart.at[tidx[d]], fpr.at[i], (e, tidx[d])) for i, d in enumerate(tens)]

    def l4():
        total = fpart[t]
        for i in range(7):
            lc["f"][i].wait_recv()
            total = total + fpr[i]
        fmine[...] = total
        feat_ref[t] = total
        lc["sib"] = cp.go(fmine, fsib, sib)
        lc["out"] = [cp.go(fmine, feat_ref.at[t], (e, tidx[d])) for d in tens]

    def l5():
        lc["sib"].wait_recv()
        gcol[0, 0] = fmine[...] + fsib[...]
        lc["x"] = [cp.go(gcol.at[0, 0], gcol.at[0, dx], xs_dev[dx]) for dx in (1, 2, 3)]

    def l6():
        for copy in lc["x"]:
            copy.wait_recv()
        lc["z"] = [cp.go(gcol.at[0], gcol.at[dz], zs_dev[dz]) for dz in (1, 2, 3)]

    def l7():
        for copy in lc["z"]:
            copy.wait_recv()
        lanes = pl.ds(pl.multiple_of((e % 4) * 128, 128), 128)
        rowb[0] = gcol[:, :, :, lanes]
        index = cp.count
        cp.count += 8
        lc["row"] = [
            pltpu.make_async_remote_copy(
                src_ref=rowb.at[0],
                dst_ref=rowb.at[1],
                send_sem=send_sems.at[index + i],
                recv_sem=recv_sems.at[index],
                device_id=(e, tidx[d]),
                device_id_type=MESH,
            )
            for i, d in enumerate(tens)
        ]

        @pl.when(t == e // 4)
        def _():
            for copy in lc["row"]:
                copy.start()
            rowb[1] = rowb[0]

    def l8():
        @pl.when(t == e // 4)
        def _():
            for copy in lc["row"]:
                copy.wait_send()

        @pl.when(t != e // 4)
        def _():
            lc["row"][0].wait_recv()

        row = rowb[1].reshape(128, 128)
        col = gcol[...].reshape(128, 512)
        gram = jnp.dot(row.T, col, precision=HIGHEST, preferred_element_type=F32) / 128.0
        rg = lax.broadcasted_iota(jnp.int32, (128, 512), 0) + e * 128
        cg = lax.broadcasted_iota(jnp.int32, (128, 512), 1) + t * 512
        hess_ref[...] = gram + DAMPING * (rg == cg).astype(F32)

    sb = [sb0, sb1, sb2, sb3]

    def kslot(yy):
        return ((yy // 2 + zh) % 2) * 2 + (yy % 2 + x // 2) % 2

    k0, kp, km, k2 = (kslot((y + d) % 4) for d in (0, 1, 3, 2))
    base = ((zh + k0 // 2) % 4) // 2
    h_own = (zl + base) % 2
    h_oth = 1 - h_own
    par = (y + x // 2 + x) % 2
    off = [sum(NT[:i]) for i in range(ROUNDS)]
    poff = [sum(len(q) for q in PAIR_TILES[:i]) for i in range(ROUNDS)]
    c1c, c2c, zc, xc = {}, {}, {}, {}

    def put(i, res, first):
        count = res.shape[1] // 128
        for k in range(4):
            for h in range(2):
                for n in range(count):
                    row0 = (k * 2 + h) * 64
                    sb[i][k, h, first + n] = res[row0 : row0 + 64, n * 128 : n * 128 + 128].astype(BF16)

    def mm(r, a_ref, rows):
        return lax.dot_general(
            wbuf[r].reshape(512, KDIM), a_ref[rows], (((1,), (1,)), ((), ())), preferred_element_type=F32
        )

    def compute(i):
        for half in range(2):
            put(i, mm(i, a_own, pl.ds(half * 256, 256)), half * 2)
        a_copy[i].wait_recv()
        for n, (r, a) in enumerate(PAIR_TILES[i]):
            put(i, mm(r, a_pair, pl.ds(a * 128, 128)), 4 + n)

    def c1(i):
        span = pl.ds(off[i], NT[i])
        c1c[i, "p"] = cp.go(sb[i].at[k2, 0], r1p.at[span], yp)
        c1c[i, "m"] = cp.go(sb[i].at[k2, 1], r1m.at[span], ym)
        c2c[i, "p1"] = cp.go(sb[i].at[kp, 1], r2m.at[1, span], yp)
        c2c[i, "m0"] = cp.go(sb[i].at[km, 0], r2p.at[0, span], ym)

    def c2(i):
        span = pl.ds(off[i], NT[i])
        c1c[i, "p"].wait_recv()
        sb[i][kp, 0] = (sb[i][kp, 0].astype(F32) + r1p[span].astype(F32)).astype(BF16)
        c2c[i, "p0"] = cp.go(sb[i].at[kp, 0], r2m.at[0, span], yp)
        c1c[i, "m"].wait_recv()
        sb[i][km, 1] = (sb[i][km, 1].astype(F32) + r1m[span].astype(F32)).astype(BF16)
        c2c[i, "m1"] = cp.go(sb[i].at[km, 1], r2p.at[1, span], ym)

    def c3(i):
        span = pl.ds(off[i], NT[i])
        for name in ("p1", "m0", "p0", "m1"):
            c2c[i, name].wait_recv()

        def total(h):
            return sb[i][k0, h].astype(F32) + r2m[h, span].astype(F32) + r2p[h, span].astype(F32)

        zs[span] = total(h_oth).astype(BF16)
        zc[i] = cp.go(zs.at[span], zr.at[span], zlp)
        sown[span] = total(h_own)

    def c4(i):
        zc[i].wait_recv()
        for n in range(4):
            done = (sown[off[i] + n] + zr[off[i] + n].astype(F32)).astype(BF16)
            o_ref[par, 0, i, :, n * 128 : n * 128 + 128] = done[:ROWS]
            o_ref[par, 1, i, :, n * 128 : n * 128 + 128] = done[ROWS:]
        count = len(PAIR_TILES[i])
        src = pl.ds(off[i] + 4, count)
        span = pl.ds(poff[i], count)
        xs[span] = (sown[src] + zr[src].astype(F32)).astype(BF16)
        xc[i] = cp.go(xs.at[span], xr.at[span], pair)

    def c5(i):
        xc[i].wait_recv()
        for n, (r, a) in enumerate(PAIR_TILES[i]):
            done = xr[poff[i] + n]
            o_ref[1 - par, 0, r, :, a * 128 : a * 128 + 128] = done[:ROWS]
            o_ref[1 - par, 1, r, :, a * 128 : a * 128 + 128] = done[ROWS:]

    s1(0)
    l3()
    s2(0)
    s3(0)
    s1(1)
    s4(0)
    compute(0)
    c1(0)
    l4()
    s2(1)
    s3(1)
    c2(0)
    s1(2)
    s4(1)
    compute(1)
    c1(1)
    l5()
    c3(0)
    s2(2)
    s3(2)
    c2(1)
    s1(3)
    s4(2)
    compute(2)
    c1(2)
    l6()
    c4(0)
    c3(1)
    s2(3)
    c2(2)
    s3(3)
    s4(3)
    compute(3)
    c1(3)
    l7()
    c4(1)
    c3(2)
    c2(3)
    l8()
    c4(2)
    c3(3)
    c5(0)
    c5(1)
    c4(3)
    c5(2)
    for copy in lc["out"]:
        copy.wait_recv()
    for copy in cp.sent:
        copy.wait_send()
    c5(3)


def body(layer_input, gate_act, hidden_grad, up_weight, proj_input, proj_output, sequence_ids):
    tiles = sum(NT)
    pair_tiles = sum(len(q) for q in PAIR_TILES)
    anyspec = pl.BlockSpec(memory_space=pl.ANY)
    vm = pl.BlockSpec(memory_space=pltpu.VMEM)
    o, feat, hess = pl.pallas_call(
        kernel,
        out_shape=(
            jax.ShapeDtypeStruct((2, 2, ROUNDS, ROWS, TOK), BF16),
            jax.ShapeDtypeStruct((8, 8, 512), F32),
            jax.ShapeDtypeStruct((128, 512), F32),
        ),
        in_specs=[anyspec] * 6 + [vm],
        out_specs=(vm, vm, vm),
        scratch_shapes=[
            pltpu.VMEM((512, 512), BF16),
            pltpu.VMEM((512, KDIM), BF16),
            pltpu.VMEM((512, KDIM), BF16),
            pltpu.VMEM((512, RANK), BF16),
            pltpu.VMEM((KDIM, RANK), BF16),
            pltpu.VMEM((512, KDIM), BF16),
            pltpu.VMEM((512, KDIM), BF16),
            pltpu.VMEM((ROUNDS, 4, 4, ROWS, KDIM), BF16),
        ]
        + [pltpu.VMEM((4, 2, NT[i], 64, 128), BF16) for i in range(ROUNDS)]
        + [
            pltpu.VMEM((tiles, 64, 128), BF16),
            pltpu.VMEM((tiles, 64, 128), BF16),
            pltpu.VMEM((2, tiles, 64, 128), BF16),
            pltpu.VMEM((2, tiles, 64, 128), BF16),
            pltpu.VMEM((tiles, 64, 128), BF16),
            pltpu.VMEM((tiles, 64, 128), BF16),
            pltpu.VMEM((tiles, 64, 128), F32),
            pltpu.VMEM((pair_tiles, 64, 128), BF16),
            pltpu.VMEM((pair_tiles, 64, 128), BF16),
            pltpu.VMEM((8, 64, 128), F32),
            pltpu.VMEM((7, 64, 128), F32),
            pltpu.VMEM((8, 8, 512), F32),
            pltpu.VMEM((7, 8, 512), F32),
            pltpu.VMEM((8, 512), F32),
            pltpu.VMEM((8, 512), F32),
            pltpu.VMEM((4, 4, 8, 512), F32),
            pltpu.VMEM((2, 4, 4, 8, 128), F32),
            pltpu.SemaphoreType.DMA((N_COPIES,)),
            pltpu.SemaphoreType.DMA((N_COPIES,)),
            pltpu.SemaphoreType.DMA((16,)),
        ],
        compiler_params=pltpu.CompilerParams(
            collective_id=0, has_side_effects=True, vmem_limit_bytes=60 * 1024 * 1024
        ),
    )(layer_input, gate_act, hidden_grad, up_weight, proj_input, proj_output, sequence_ids.reshape(8, 64))
    input_grad = o.reshape(512, TOK).T
    features = (feat[:, :4] + feat[:, 4:]).transpose(1, 0, 2).reshape(4, 4096)
    return input_grad, features, hess


def solution(mesh):
    return jax.shard_map(
        body,
        mesh=mesh,
        in_specs=(
            P("example", "tensor"),
            P("example", "tensor"),
            P("example", "tensor"),
            P("example", "tensor"),
            P("tensor", None),
            P("tensor", None),
            P("example"),
        ),
        out_specs=(P("example", "tensor"), P("example", None), P("example", "tensor")),
        check_vma=False,
    )
```

time: 273 us -> 115 us (0.42)
  the two profiles are of different devices: /device:TPU:1 before, /device:TPU:42 now
where the time goes in v1:
time: 115 us
  Pallas kernels  104 us (90%)
  local copies, waits for them, and re-layouts  8.58 us (7%)
  other arithmetic  1.63 us (1%)
    pallas_call x1, Pallas kernels, body(): pl.pallas_call(kernel, out_shape=(jax.ShapeDtypeStruct((2, 2, ROUNDS, ROW...  104 us
    unnamed x3, local copies, waits for them, and re-layouts  5.18 us

profile of v1, /device:TPU:42, one launch (start us, length us, event | category | flops | bytes accessed | tf_op | source)
XLA Modules:
  0.0 115.2 jit_solution(8403147548523329105)
XLA Ops:
  0.6 1.3 %reshape.15.ids_ref = s32[8,64]{1,0:T(8,128)} reshape(s32[512]{0:T(512)} %param.13) | data formatting | bytes 4096 | tf_op jit(solution)/shard_map/reshape | solution.py:449
  2.0 1.6 %copy.10.pi_in = bf16[512,64]{1,0:T(8,128)(2,1)} copy(bf16[512,64]{0,1:T(8,128)(2,1)} %param.11) | data formatting | bytes 131072 | tf_op args[4]
  3.6 1.9 %copy.11.po_in = bf16[1792,64]{1,0:T(8,128)(2,1)} copy(bf16[1792,64]{0,1:T(8,128)(2,1)} %param.12) | data formatting | bytes 458752 | tf_op args[5]
  5.5 104.3 %shard_map.94 = (bf16[2,2,4,32,512]{4,3,2,1,0:T(8,128)(2,1)}, f32[8,8,512]{2,1,0:T(8,128)}, f32[128,512]{1,0:T(8,128)}) custom-call(bf16[512,512]{1,0:T(8,128)(2,1)} %x_in.1, bf16[512,1792]{1,0:T(8,128)(2,1)} %gate_in.1, bf16[512,1792]{1,0:T(8,128)(2,1)} %hid_in.1, bf16[128,1792]{1,0:T(8,128)(2,1)} %w_in.1, bf16[512,64]{1,0:T(8,128)(2,1)} %copy.10.pi_in, ...), custom_call_target="tpu_custom_call" | custom-call | tf_op jit(solution)/shard_map/pallas_call | solution.py:404
  109.8 2.0 %copy.12 = bf16[512,512]{0,1:T(8,128)(2,1)} copy(bf16[512,512]{1,0:T(8,128)(2,1)} %bitcast.6) | data formatting | bytes 1048576 | tf_op jit(solution)/shard_map/reshape | solution.py:450
  111.9 1.6 %slice_add_fusion = f32[8,4,512]{2,1,0:T(4,128)} fusion(f32[8,8,512]{2,1,0:T(8,128)} %get-tuple-element.7), kind=kLoop, calls=%fused_computation | loop fusion | flops 16384 | bytes 196608 | tf_op jit(solution)/shard_map/add | solution.py:451
  113.5 1.7 %copy.14 = f32[128,512]{1,0:T(8,128)} copy(f32[128,512]{1,0:T(8,128)} %get-tuple-element.14) | data formatting | bytes 524288

commit v2 on v1

v2 whole, which is shorter than its diff:
```python
import jax
import jax.numpy as jnp
from jax import lax
from jax.experimental import pallas as pl
from jax.experimental.pallas import tpu as pltpu
from jax.sharding import PartitionSpec as P

MESH = pl.DeviceIdType.MESH
F32 = jnp.float32
BF16 = jnp.bfloat16
LAST = (((1,), (1,)), ((), ()))
HIGHEST = lax.Precision.HIGHEST

DAMPING = 0.1
TOK = 512
KDIM = 1792
RANK = 64
ROUNDS = 8
ROWS = 16
SUB = 2 * ROWS
OWN_X, OWN_Z = 8, 3
PLAN = (
    ("0o", "00"),
    ("1o", "10"),
    ("2o", "20", "21", "01", "11"),
    ("3o", "30", "31"),
    ("4o", "40", "41", "42", "02", "12", "22", "32"),
    ("5o", "50", "51", "52"),
    ("03", "13", "23", "33", "43", "53"),
    ("6o", "60", "61", "62", "63"),
    ("7o", "70", "71", "72", "73"),
)


def tiles_of(text):
    own, other = [], []
    for word in text:
        if word[1] == "o":
            own += [("own", int(word[0]), n) for n in range(4)]
        else:
            other.append(("pair", int(word[0]), int(word[1])))
    return own, other


OWNS = [tiles_of(text)[0] for text in PLAN]
PAIRS = [tiles_of(text)[1] for text in PLAN]
BATCHES = [o + p for o, p in zip(OWNS, PAIRS)]
NB = len(BATCHES)
LATE = 8
NT = [len(q) for q in BATCHES]
NP = [len(q) for q in PAIRS]

STEPS = (
    "s10", "s11", "l2", "s20", "s12", "l3", "s30", "s21", "s13", "s40", "mm0", "c10",
    "l4", "s31", "s22", "s14", "s41", "mm1", "c11", "c20", "l5", "s32", "s23", "s15",
    "s42", "mm2", "c12", "c21", "l6", "s33", "s24", "s16", "s43", "mm3", "c13", "c22",
    "c30", "l7", "s34", "s25", "s17", "s44", "mm4", "c14", "c23", "c31", "l8", "s26",
    "s35", "s45", "mm5", "c15", "c24", "c32", "l9", "s27", "mm6", "c16", "c25", "c33",
    "c40", "c41", "s36", "s46", "mm7", "c17", "c26", "c34", "c42", "c43", "s37", "c35",
    "c44", "s47", "mm8", "c18", "c27", "c36", "c45", "c28", "c37", "c46", "c38", "c47",
    "c50", "c51", "c52", "c53", "c54", "c55", "c56", "c57", "c48", "la", "c58",
)


class Copies:
    def __init__(self, send_sems, recv_sems):
        self.send, self.recv, self.count, self.sent = send_sems, recv_sems, 0, []

    def make(self, src, dst, device):
        index = self.count
        self.count += 1
        copy = pltpu.make_async_remote_copy(
            src_ref=src,
            dst_ref=dst,
            send_sem=self.send.at[index],
            recv_sem=self.recv.at[index],
            device_id=device,
            device_id_type=MESH,
        )
        return copy

    def go(self, src, dst, device):
        copy = self.make(src, dst, device)
        copy.start()
        self.sent.append(copy)
        return copy


N_COPIES = 300


def kernel(
    x_in, gate_in, hid_in, w_in, pi_in, po_in, ids_ref,
    o_ref, feat_ref, gcol, rowb,
    xv, gv, hv, piv, pov, a_own, a_pair, wbuf,
    sb, r1p, r1m, r2m, r2p, zs, zr, sown, xs, xr, xr2,
    low, lowr, lowz, fpart, fpr, fz, fsib,
    send_sems, recv_sems, loc_sems,
):
    e = lax.axis_index("example")
    t = lax.axis_index("tensor")
    zh, x, c = e // 8, (e // 2) % 4, e % 2
    zl, y = t // 4, t % 4

    def ex(zh_, x_, c_):
        return zh_ * 8 + x_ * 2 + c_

    def te(zl_, y_):
        return zl_ * 4 + y_

    sib = (ex(zh, x, 1 - c), t)
    pair = (ex(zh, x + 1 - 2 * (x % 2), c), t)
    pairz = (ex(zh, x + 1 - 2 * (x % 2), c), te(1 - zl, y))
    qdev = (ex(zh, 3 - x, c), t)
    zp = (ex((zh + 1) % 4, x, c), t)
    zm = (ex((zh + 3) % 4, x, c), t)
    yp = (e, te(zl, (y + 1) % 4))
    ym = (e, te(zl, (y + 3) % 4))
    zlp = (e, te(1 - zl, y))
    xs_dev = {dx: (ex(zh, (x + dx) % 4, c), t) for dx in (1, 2, 3)}
    zs_dev = {dz: (ex((zh + dz) % 4, x, c), t) for dz in (1, 2, 3)}
    y_dev = {d: (e, te(zl, (y + d) % 4)) for d in (1, 2, 3)}
    tens = [(dzl, dy) for dzl in range(2) for dy in range(4) if (dzl, dy) != (0, 0)]
    tidx = {d: te((zl + d[0]) % 2, (y + d[1]) % 4) for d in tens}

    barrier = pltpu.get_barrier_semaphore()
    partners = [sib, pairz] + list(xs_dev.values()) + list(zs_dev.values()) + [(e, tidx[d]) for d in tens]
    for dev in partners:
        pl.semaphore_signal(barrier, inc=1, device_id=dev, device_id_type=MESH)

    loads = []

    def load(src, dst):
        copy = pltpu.make_async_copy(src, dst, loc_sems.at[len(loads)])
        copy.start()
        loads.append(copy)
        return copy

    w_load = [load(w_in.at[pl.ds(r * ROWS, ROWS)], wbuf.at[r, 0, c]) for r in range(ROUNDS)]
    gh_load = []
    for a in range(4):
        rows = pl.ds(a * 128, 128)
        gh_load.append((load(gate_in.at[rows], gv.at[rows]), load(hid_in.at[rows], hv.at[rows])))
    low_load = [load(x_in, xv), load(pi_in, piv), load(po_in, pov)]

    pl.semaphore_wait(barrier, len(partners))
    cp = Copies(send_sems, recv_sems)

    def slot(r, dz, s, core):
        return wbuf.at[r, (dz % 2) * 2 + s, (dz // 2) * 2 + core]

    w_z = {}
    w_x = {}
    w_s = {}

    def own_z(r):
        if r < ROUNDS:
            w_z[r, 3] = cp.go(slot(r, 0, 0, c), slot(r, 3, 0, c), zp)
            w_z[r, 1] = cp.go(slot(r, 0, 0, c), slot(r, 1, 0, c), zm)

    def own_x(r):
        if r < ROUNDS:
            w_x[r, 0] = cp.go(slot(r, 0, 0, c), slot(r, 0, 1, c), qdev)

    def own_s(r):
        w_s[r, 0, 0] = cp.go(slot(r, 0, 0, c), slot(r, 0, 0, c), sib)

    def s1(r):
        w_z[r, 3].wait_recv()
        if r % 2 == 0:
            w_z[r, 2] = cp.go(slot(r, 3, 0, c), slot(r, 2, 0, c), zp)
        w_x[r, 3] = cp.go(slot(r, 3, 0, c), slot(r, 3, 1, c), qdev)
        w_z[r, 1].wait_recv()
        if r % 2 == 1:
            w_z[r, 2] = cp.go(slot(r, 1, 0, c), slot(r, 2, 0, c), zm)
        w_x[r, 1] = cp.go(slot(r, 1, 0, c), slot(r, 1, 1, c), qdev)
        own_z(r + OWN_Z)
        own_x(r + OWN_X)
        w_s[r, 3, 0] = cp.go(slot(r, 3, 0, c), slot(r, 3, 0, c), sib)
        w_s[r, 1, 0] = cp.go(slot(r, 1, 0, c), slot(r, 1, 0, c), sib)

    def s2(r):
        w_z[r, 2].wait_recv()
        w_x[r, 2] = cp.go(slot(r, 2, 0, c), slot(r, 2, 1, c), qdev)
        w_s[r, 2, 0] = cp.go(slot(r, 2, 0, c), slot(r, 2, 0, c), sib)

    def s3(r):
        for dz in (0, 3, 1, 2):
            w_x[r, dz].wait_recv()
            w_s[r, dz, 1] = cp.go(slot(r, dz, 1, c), slot(r, dz, 1, c), sib)

    def s4(r):
        for dz in (0, 3, 1, 2):
            for s in range(2):
                w_s[r, dz, s].wait_recv()

    for r in range(ROUNDS):
        w_load[r].wait()
        if r < OWN_Z:
            own_z(r)
        if r < OWN_X:
            own_x(r)
    for r in range(ROUNDS):
        own_s(r)

    a_copy = []
    for a in range(4):
        for copy in gh_load[a]:
            copy.wait()

        def up(j, _, a=a):
            rows = pl.ds(a * 128 + j * 16, 16)
            g = gv[rows].astype(F32)
            h = hv[rows].astype(F32)
            a_own[rows] = (h * (g / (1.0 + jnp.exp(-g)))).astype(BF16)
            return 0

        lax.fori_loop(0, 8, up, 0)
        rows = pl.ds(a * 128, 128)
        a_copy.append(cp.go(a_own.at[rows], a_pair.at[rows], pair))

    for copy in low_load:
        copy.wait()
    for n in range(4):
        rows = pl.ds(n * 128, 128)
        one = lax.dot_general(xv[rows], piv[...], LAST, preferred_element_type=F32)
        two = lax.dot_general(a_own[rows], pov[...], LAST, preferred_element_type=F32)
        both = jnp.concatenate([one, two], axis=1)
        low[(2 * n) % 4, n // 2] = both[:64]
        low[(2 * n + 1) % 4, n // 2] = both[64:]
    lc = {"a": [cp.go(low.at[(y + d) % 4], lowr.at[d - 1], y_dev[d]) for d in (1, 2, 3)]}

    def l2():
        for copy in lc["a"]:
            copy.wait_recv()
        lowz[0] = low[y, 1 - zl] + lowr[0, 1 - zl] + lowr[1, 1 - zl] + lowr[2, 1 - zl]
        lc["b"] = cp.go(lowz.at[0], lowz.at[1], zlp)
        lowz[2] = low[y, zl] + lowr[0, zl] + lowr[1, zl] + lowr[2, zl]

    def l3():
        lc["b"].wait_recv()
        total = lowz[1] + lowz[2]
        lane = lax.broadcasted_iota(jnp.int32, (64, 128), 1)
        out2 = jnp.where(lane < 64, pltpu.roll(total, 64, 1), total)
        local = ids_ref[...] - 4 * e + 4 * c
        hot = (lax.broadcasted_iota(jnp.int32, (8, 512), 0) == local).astype(F32)
        hot = pltpu.roll(hot, (8 - t) % 8 * 64, 1)[:, :64] * ((4 / 512) ** 0.5)
        sides = jnp.concatenate([total, jnp.zeros((64, 128), F32)], axis=0).T[:64, :64]
        left = (sides[:, None, :] * hot[None, :, :]).reshape(512, 64)
        grads = jnp.dot(left, out2, precision=HIGHEST, preferred_element_type=F32).reshape(64, 8, 128)
        low_half = lax.broadcasted_iota(jnp.int32, (8, 128), 1) < 64
        for j in range(32):
            part = jnp.where(low_half, grads[2 * j], grads[2 * j + 1])
            fpart[(j // 4) % 4, j // 16, :, (j % 4) * 128 : (j % 4) * 128 + 128] = part
        lc["c"] = [cp.go(fpart.at[(y + d) % 4], fpr.at[d - 1], y_dev[d]) for d in (1, 2, 3)]

    def l4():
        for copy in lc["c"]:
            copy.wait_recv()
        oth = 1 - zl
        fz[0] = fpart[y, oth] + fpr[0, oth] + fpr[1, oth] + fpr[2, oth]
        lc["d"] = cp.go(fz.at[0], fz.at[1], zlp)
        fz[2] = fpart[y, zl] + fpr[0, zl] + fpr[1, zl] + fpr[2, zl]

    def l5():
        lc["d"].wait_recv()
        mine = fz[1] + fz[2]
        halves = [jnp.concatenate([mine[:, q : q + 128], mine[:, q + 128 : q + 256]], axis=0) for q in (0, 256)]
        keep = jnp.where(c == 0, halves[0], halves[1])
        fsib[0] = jnp.where(c == 0, halves[1], halves[0])
        fsib[2] = keep
        lc["sib"] = cp.go(fsib.at[0], fsib.at[1], sib)
        feat_ref[y, zl] = mine
        lc["o1"] = cp.go(feat_ref.at[y, zl], feat_ref.at[y, zl], zlp)

    def l6():
        lc["sib"].wait_recv()
        gcol[c, 0, 0] = (fsib[1] + fsib[2]).astype(BF16)
        lc["x"] = [cp.go(gcol.at[c, 0, 0], gcol.at[c, 0, dx], xs_dev[dx]) for dx in (1, 2, 3)]
        lc["o1"].wait_recv()
        lc["out"] = [cp.go(feat_ref.at[y], feat_ref.at[y], y_dev[d]) for d in (1, 2, 3)]

    def l7():
        for copy in lc["x"]:
            copy.wait_recv()
        lc["z"] = [cp.go(gcol.at[c, 0], gcol.at[c, dz], zs_dev[dz]) for dz in (1, 2, 3)]

    def l8():
        for copy in lc["z"]:
            copy.wait_recv()
        lc["half"] = cp.go(gcol.at[c], gcol.at[c], sib)

    def l9():
        lc["half"].wait_recv()
        both = gcol[(e // 2) % 2].astype(F32)
        first = both[:, :, :8].reshape(128, 128)
        rowb[0] = jnp.where(e % 2 == 0, first, both[:, :, 8:].reshape(128, 128)).astype(BF16)
        index = cp.count
        cp.count += 8
        lc["row"] = [
            pltpu.make_async_remote_copy(
                src_ref=rowb.at[0],
                dst_ref=rowb.at[1],
                send_sem=send_sems.at[index + i],
                recv_sem=recv_sems.at[index],
                device_id=(e, tidx[d]),
                device_id_type=MESH,
            )
            for i, d in enumerate(tens)
        ]

        @pl.when(t == e // 4)
        def _():
            for copy in lc["row"]:
                copy.start()
            rowb[1] = rowb[0]

    def la():
        @pl.when(t == e // 4)
        def _():
            for copy in lc["row"]:
                copy.wait_send()

        @pl.when(t != e // 4)
        def _():
            lc["row"][0].wait_recv()

    def kslot(yy):
        return ((yy // 2 + zh) % 2) * 2 + (yy % 2 + x // 2) % 2

    k0, kp, km, k2 = (kslot((y + d) % 4) for d in (0, 1, 3, 2))
    base = ((zh + k0 // 2) % 4) // 2
    h_own = (zl + base) % 2
    h_oth = 1 - h_own
    par = (y + x // 2 + x) % 2
    off = [sum(NT[:i]) for i in range(NB)]
    poff = [sum(NP[:i]) for i in range(NB)]
    c1c, c2c, zc, xc = {}, {}, {}, {}

    def mm(w, a_ref, rows):
        return lax.dot_general(w, a_ref[rows], LAST, preferred_element_type=F32)

    def put(res, n):
        for k in range(4):
            for h in range(2):
                row0 = (k * 2 + h) * SUB
                sb[k, h, n] = res[row0 : row0 + SUB].astype(BF16)

    waited = set()

    def compute(i):
        w = {}
        tiles = BATCHES[i]
        n = 0
        while n < len(tiles):
            kind, r, chunk = tiles[n]
            if kind == "pair" and chunk not in waited:
                waited.add(chunk)
                a_copy[chunk].wait_recv()
            wide = 2 if n + 1 < len(tiles) and tiles[n + 1] == (kind, r, chunk + 1) and chunk % 2 == 0 else 1
            if wide == 2 and kind == "pair" and chunk + 1 not in waited:
                waited.add(chunk + 1)
                a_copy[chunk + 1].wait_recv()
            src = a_own if kind == "own" else a_pair
            res = mm(wbuf[r].reshape(16 * ROWS, KDIM), src, pl.ds(chunk * 128, 128 * wide))
            for q in range(wide):
                put(res[:, q * 128 : q * 128 + 128], off[i] + n + q)
            n += wide

    def c1(i):
        span = pl.ds(off[i], NT[i])
        c1c[i, "p"] = cp.go(sb.at[k2, 0, span], r1p.at[span], yp)
        c1c[i, "m"] = cp.go(sb.at[k2, 1, span], r1m.at[span], ym)
        c2c[i, "p1"] = cp.go(sb.at[kp, 1, span], r2m.at[1, span], yp)
        c2c[i, "m0"] = cp.go(sb.at[km, 0, span], r2p.at[0, span], ym)

    def c2(i):
        span = pl.ds(off[i], NT[i])
        c1c[i, "p"].wait_recv()
        sb[kp, 0, span] = (sb[kp, 0, span].astype(F32) + r1p[span].astype(F32)).astype(BF16)
        c2c[i, "p0"] = cp.go(sb.at[kp, 0, span], r2m.at[0, span], yp)
        c1c[i, "m"].wait_recv()
        sb[km, 1, span] = (sb[km, 1, span].astype(F32) + r1m[span].astype(F32)).astype(BF16)
        c2c[i, "m1"] = cp.go(sb.at[km, 1, span], r2p.at[1, span], ym)

    def c3(i):
        span = pl.ds(off[i], NT[i])
        for name in ("p1", "m0", "p0", "m1"):
            c2c[i, name].wait_recv()

        def total(h, span):
            return sb[k0, h, span].astype(F32) + r2m[h, span].astype(F32) + r2p[h, span].astype(F32)

        if i < LATE:
            zs[span] = total(h_oth, span).astype(BF16)
            zc[i] = cp.go(zs.at[span], zr.at[span], zlp)
            sown[span] = total(h_own, span)
            return
        owns = len(OWNS[i])
        osrc, psrc = pl.ds(off[i], owns), pl.ds(off[i] + owns, NP[i])
        pspan, lspan = pl.ds(poff[i], NP[i]), pl.ds(poff[i] - poff[LATE], NP[i])
        zs[psrc] = total(h_oth, psrc).astype(BF16)
        xc[i, 2] = cp.go(zs.at[psrc], xr2.at[lspan], pairz)
        zs[osrc] = total(h_oth, osrc).astype(BF16)
        zc[i] = cp.go(zs.at[osrc], zr.at[osrc], zlp)
        xs[pspan] = total(h_own, psrc).astype(BF16)
        xc[i] = cp.go(xs.at[pspan], xr.at[pspan], pair)
        sown[osrc] = total(h_own, osrc)

    def c4(i):
        owns = len(OWNS[i])
        zc[i].wait_recv()
        if NP[i] and i < LATE:
            src = pl.ds(off[i] + owns, NP[i])
            span = pl.ds(poff[i], NP[i])
            xs[span] = (sown[src] + zr[src].astype(F32)).astype(BF16)
            xc[i] = cp.go(xs.at[span], xr.at[span], pair)
        for n, (_, r, a) in enumerate(OWNS[i]):
            done = (sown[off[i] + n] + zr[off[i] + n].astype(F32)).astype(BF16)
            o_ref[par, 0, r, :, a * 128 : a * 128 + 128] = done[:ROWS]
            o_ref[par, 1, r, :, a * 128 : a * 128 + 128] = done[ROWS:]

    def c5(i):
        if NP[i]:
            xc[i].wait_recv()
        if i >= LATE:
            xc[i, 2].wait_recv()
        for n, (_, r, a) in enumerate(PAIRS[i]):
            done = xr[poff[i] + n]
            if i >= LATE:
                more = xr2[poff[i] - poff[LATE] + n]
                done = (done.astype(F32) + more.astype(F32)).astype(BF16)
            o_ref[1 - par, 0, r, :, a * 128 : a * 128 + 128] = done[:ROWS]
            o_ref[1 - par, 1, r, :, a * 128 : a * 128 + 128] = done[ROWS:]

    table = {
        "s1": s1, "s2": s2, "s3": s3, "s4": s4, "mm": compute,
        "c1": c1, "c2": c2, "c3": c3, "c4": c4, "c5": c5,
        "l3": l3, "l4": l4, "l5": l5, "l6": l6, "l7": l7, "l8": l8, "l9": l9, "la": la, "l2": l2,
    }
    for step in STEPS:
        if step[0] == "l":
            table[step]()
        else:
            table[step[:2]](int(step[2:]))
    for copy in lc["out"]:
        copy.wait_recv()
    for copy in cp.sent:
        copy.wait_send()


def finish(o_ref, feat_ref, gcol, rowb, grad_ref, out_ref, hess_ref):
    e = lax.axis_index("example")
    t = lax.axis_index("tensor")
    for q in range(4):
        rows = slice(q * 128, q * 128 + 128)
        grad_ref[:, rows] = o_ref[rows].astype(F32).T.astype(BF16)
    for yy in range(4):
        for zz in range(2):
            both = feat_ref[yy, zz]
            first = (zz * 4 + yy) * 512
            out_ref[:, first : first + 512] = both[:4] + both[4:]
    parts = []
    for q in range(4):
        part = gcol[q // 2, :, :, (q % 2) * 8 : (q % 2) * 8 + 8]
        parts.append(part.astype(F32).reshape(128, 128))
    col = jnp.concatenate(parts, axis=1).astype(BF16)
    gram = jnp.dot(rowb[1].astype(F32).T.astype(BF16), col, preferred_element_type=F32) / 128.0
    rg = lax.broadcasted_iota(jnp.int32, (128, 512), 0) + e * 128
    cg = lax.broadcasted_iota(jnp.int32, (128, 512), 1) + t * 512
    hess_ref[...] = gram + DAMPING * (rg == cg).astype(F32)


def body(layer_input, gate_act, hidden_grad, up_weight, proj_input, proj_output, sequence_ids):
    tiles = sum(NT)
    pair_tiles = sum(NP)
    anyspec = pl.BlockSpec(memory_space=pl.ANY)
    vm = pl.BlockSpec(memory_space=pltpu.VMEM)
    o, feat, gcol, rowb = pl.pallas_call(
        kernel,
        out_shape=(
            jax.ShapeDtypeStruct((2, 2, ROUNDS, ROWS, TOK), BF16),
            jax.ShapeDtypeStruct((4, 2, 8, 512), F32),
            jax.ShapeDtypeStruct((2, 4, 4, 16, 128), BF16),
            jax.ShapeDtypeStruct((2, 128, 128), BF16),
        ),
        in_specs=[anyspec] * 6 + [vm],
        out_specs=(vm, vm, vm, vm),
        scratch_shapes=[
            pltpu.VMEM((512, 512), BF16),
            pltpu.VMEM((512, KDIM), BF16),
            pltpu.VMEM((512, KDIM), BF16),
            pltpu.VMEM((RANK, 512), BF16),
            pltpu.VMEM((RANK, KDIM), BF16),
            pltpu.VMEM((512, KDIM), BF16),
            pltpu.VMEM((512, KDIM), BF16),
            pltpu.VMEM((ROUNDS, 4, 4, ROWS, KDIM), BF16),
        ]
        + [pltpu.VMEM((4, 2, tiles, SUB, 128), BF16)]
        + [
            pltpu.VMEM((tiles, SUB, 128), BF16),
            pltpu.VMEM((tiles, SUB, 128), BF16),
            pltpu.VMEM((2, tiles, SUB, 128), BF16),
            pltpu.VMEM((2, tiles, SUB, 128), BF16),
            pltpu.VMEM((tiles, SUB, 128), BF16),
            pltpu.VMEM((tiles, SUB, 128), BF16),
            pltpu.VMEM((tiles, SUB, 128), F32),
            pltpu.VMEM((pair_tiles, SUB, 128), BF16),
            pltpu.VMEM((pair_tiles, SUB, 128), BF16),
            pltpu.VMEM((sum(NP[LATE:]), SUB, 128), BF16),
            pltpu.VMEM((4, 2, 64, 128), F32),
            pltpu.VMEM((3, 2, 64, 128), F32),
            pltpu.VMEM((3, 64, 128), F32),
            pltpu.VMEM((4, 2, 8, 512), F32),
            pltpu.VMEM((3, 2, 8, 512), F32),
            pltpu.VMEM((3, 8, 512), F32),
            pltpu.VMEM((3, 16, 128), F32),
            pltpu.SemaphoreType.DMA((N_COPIES,)),
            pltpu.SemaphoreType.DMA((N_COPIES,)),
            pltpu.SemaphoreType.DMA((24,)),
        ],
        compiler_params=pltpu.CompilerParams(
            collective_id=0, has_side_effects=True, vmem_limit_bytes=60 * 1024 * 1024
        ),
    )(layer_input, gate_act, hidden_grad, up_weight, proj_input.T, proj_output.T, sequence_ids.reshape(1, 512))
    return pl.pallas_call(
        finish,
        out_shape=(
            jax.ShapeDtypeStruct((TOK, 512), BF16),
            jax.ShapeDtypeStruct((4, 4096), F32),
            jax.ShapeDtypeStruct((128, 512), F32),
        ),
        in_specs=[vm] * 4,
        out_specs=(vm, vm, vm),
    )(o.reshape(512, TOK), feat, gcol, rowb)


def solution(mesh):
    return jax.shard_map(
        body,
        mesh=mesh,
        in_specs=(
            P("example", "tensor"),
            P("example", "tensor"),
            P("example", "tensor"),
            P("example", "tensor"),
            P("tensor", None),
            P("tensor", None),
            P("example"),
        ),
        out_specs=(P("example", "tensor"), P("example", None), P("example", "tensor")),
        check_vma=False,
    )
```

time: 115 us -> 96.2 us (0.84)
  the two profiles are of different devices: /device:TPU:42 before, /device:TPU:1 now
where the time goes in v2:
time: 96.2 us; the launch traced here: 96 us
  Pallas kernels  95.4 us (99%)
    pallas_call x1, Pallas kernels, body(): pl.pallas_call(kernel, out_shape=(jax.ShapeDtypeStruct((2, 2, ROUNDS, ROW...  93.1 us
    pallas_call x1, Pallas kernels, body(): pl.pallas_call(finish, out_shape=(jax.ShapeDtypeStruct((TOK, 512), BF16),...  2.29 us

profile of v2, /device:TPU:1, one launch (start us, length us, event | category | flops | bytes accessed | tf_op | source)
XLA Modules:
  0.0 96.0 jit_solution(16448782479143487639)
XLA Ops:
  0.6 93.1 %shard_map.94 = (bf16[2,2,8,16,512]{4,3,2,1,0:T(8,128)(2,1)}, f32[4,2,8,512]{3,2,1,0:T(8,128)}, bf16[2,4,4,16,128]{4,3,2,1,0:T(8,128)(2,1)}, bf16[2,128,128]{2,1,0:T(8,128)(2,1)}) custom-call(bf16[512,512]{1,0:T(8,128)(2,1)} %x_in.1, bf16[512,1792]{1,0:T(8,128)(2,1)} %gate_in.1, bf16[512,1792]{1,0:T(8,128)(2,1)} %hid_in.1, bf16[128,1792]{1,0:T(8,128)(2,1)} %w_in.1, ...), custom_call_target="tpu_custom_call" | custom-call | tf_op jit(solution)/shard_map/pallas_call | solution.py:479
  93.7 2.3 %shard_map.95 = (bf16[512,512]{1,0:T(8,128)(2,1)}, f32[4,4096]{1,0:T(4,128)}, f32[128,512]{1,0:T(8,128)}) custom-call(bf16[512,512]{1,0:T(8,128)(2,1)} %bitcast.4, f32[4,2,8,512]{3,2,1,0:T(8,128)} %get-tuple-element.8.feat_ref, bf16[2,4,4,16,128]{4,3,2,1,0:T(8,128)(2,1)} %get-tuple-element.9.gcol, bf16[2,128,128]{2,1,0:T(8,128)(2,1)} %get-tuple-element.10.rowb), custom_call_target="tpu_custom_call" | custom-call | tf_op jit(solution)/shard_map/pallas_call | solution.py:526

commit v3 on v2

--- a/solution.py
+++ b/solution.py
@@ -18,7 +18,7 @@
 ROUNDS = 8
 ROWS = 16
 SUB = 2 * ROWS
-OWN_X, OWN_Z = 8, 3
+OWN_X, OWN_Z = 4, 3
 PLAN = (
     ("0o", "00"),
     ("1o", "10"),
@@ -28,7 +28,8 @@
     ("5o", "50", "51", "52"),
     ("03", "13", "23", "33", "43", "53"),
     ("6o", "60", "61", "62", "63"),
-    ("7o", "70", "71", "72", "73"),
+    ("70", "71", "72", "73"),
+    ("7o",),
 )
 
 
@@ -51,14 +52,15 @@
 NP = [len(q) for q in PAIRS]
 
 STEPS = (
-    "s10", "s11", "l2", "s20", "s12", "l3", "s30", "s21", "s13", "s40", "mm0", "c10",
-    "l4", "s31", "s22", "s14", "s41", "mm1", "c11", "c20", "l5", "s32", "s23", "s15",
-    "s42", "mm2", "c12", "c21", "l6", "s33", "s24", "s16", "s43", "mm3", "c13", "c22",
-    "c30", "l7", "s34", "s25", "s17", "s44", "mm4", "c14", "c23", "c31", "l8", "s26",
-    "s35", "s45", "mm5", "c15", "c24", "c32", "l9", "s27", "mm6", "c16", "c25", "c33",
-    "c40", "c41", "s36", "s46", "mm7", "c17", "c26", "c34", "c42", "c43", "s37", "c35",
-    "c44", "s47", "mm8", "c18", "c27", "c36", "c45", "c28", "c37", "c46", "c38", "c47",
-    "c50", "c51", "c52", "c53", "c54", "c55", "c56", "c57", "c48", "la", "c58",
+    "s10", "s11", "s20", "s12", "l2", "s30", "s21", "s40", "mm0", "c10", "s13", "l3",
+    "s31", "s22", "s14", "s41", "mm1", "c11", "c20", "l4", "s32", "s23", "s15", "s42",
+    "mm2", "c12", "c21", "l5", "s33", "s24", "s16", "s43", "mm3", "c13", "c22", "c30",
+    "l6", "s34", "s25", "s17", "s44", "mm4", "c14", "c23", "c31", "l7", "s26", "s35",
+    "s45", "mm5", "c15", "c24", "c32", "l8", "s27", "mm6", "c16", "c25", "c33", "c40",
+    "c41", "s36", "s46", "mm7", "c17", "c26", "c34", "c42", "c43", "l9", "s37", "c35",
+    "c44", "s47", "mm8", "c18", "mm9", "c27", "c19", "c36", "c45", "c28", "c37", "c46",
+    "c29", "c38", "c47", "c39", "c50", "c51", "c52", "c53", "c54", "c55", "c56", "c57",
+    "c49", "la", "c58",
 )
 
 
@@ -136,7 +138,7 @@
         loads.append(copy)
         return copy
 
-    w_load = [load(w_in.at[pl.ds(r * ROWS, ROWS)], wbuf.at[r, 0, c]) for r in range(ROUNDS)]
+    w_load = [load(w_in.at[pl.ds(r * ROWS, ROWS)], wbuf.at[r, 0, 0, c]) for r in range(ROUNDS)]
     gh_load = []
     for a in range(4):
         rows = pl.ds(a * 128, 128)
@@ -147,7 +149,10 @@
     cp = Copies(send_sems, recv_sems)
 
     def slot(r, dz, s, core):
-        return wbuf.at[r, (dz % 2) * 2 + s, (dz // 2) * 2 + core]
+        return wbuf.at[r, (dz % 2) * 2 + s, dz // 2, core]
+
+    def slots(r, dz, s, core):
+        return wbuf.at[r, dz * 2 + s, :, core]
 
     w_z = {}
     w_x = {}
@@ -162,35 +167,32 @@
         if r < ROUNDS:
             w_x[r, 0] = cp.go(slot(r, 0, 0, c), slot(r, 0, 1, c), qdev)
 
-    def own_s(r):
-        w_s[r, 0, 0] = cp.go(slot(r, 0, 0, c), slot(r, 0, 0, c), sib)
-
     def s1(r):
         w_z[r, 3].wait_recv()
         if r % 2 == 0:
             w_z[r, 2] = cp.go(slot(r, 3, 0, c), slot(r, 2, 0, c), zp)
-        w_x[r, 3] = cp.go(slot(r, 3, 0, c), slot(r, 3, 1, c), qdev)
         w_z[r, 1].wait_recv()
         if r % 2 == 1:
             w_z[r, 2] = cp.go(slot(r, 1, 0, c), slot(r, 2, 0, c), zm)
-        w_x[r, 1] = cp.go(slot(r, 1, 0, c), slot(r, 1, 1, c), qdev)
         own_z(r + OWN_Z)
+        w_x[r, 1] = cp.go(slots(r, 1, 0, c), slots(r, 1, 1, c), qdev)
         own_x(r + OWN_X)
-        w_s[r, 3, 0] = cp.go(slot(r, 3, 0, c), slot(r, 3, 0, c), sib)
-        w_s[r, 1, 0] = cp.go(slot(r, 1, 0, c), slot(r, 1, 0, c), sib)
+        w_s[r, 1, 0] = cp.go(slots(r, 1, 0, c), slots(r, 1, 0, c), sib)
 
     def s2(r):
         w_z[r, 2].wait_recv()
         w_x[r, 2] = cp.go(slot(r, 2, 0, c), slot(r, 2, 1, c), qdev)
-        w_s[r, 2, 0] = cp.go(slot(r, 2, 0, c), slot(r, 2, 0, c), sib)
+        w_s[r, 0, 0] = cp.go(slots(r, 0, 0, c), slots(r, 0, 0, c), sib)
 
     def s3(r):
-        for dz in (0, 3, 1, 2):
-            w_x[r, dz].wait_recv()
-            w_s[r, dz, 1] = cp.go(slot(r, dz, 1, c), slot(r, dz, 1, c), sib)
+        w_x[r, 1].wait_recv()
+        w_s[r, 1, 1] = cp.go(slots(r, 1, 1, c), slots(r, 1, 1, c), sib)
+        w_x[r, 0].wait_recv()
+        w_x[r, 2].wait_recv()
+        w_s[r, 0, 1] = cp.go(slots(r, 0, 1, c), slots(r, 0, 1, c), sib)
 
     def s4(r):
-        for dz in (0, 3, 1, 2):
+        for dz in (1, 0):
             for s in range(2):
                 w_s[r, dz, s].wait_recv()
 
@@ -200,8 +202,6 @@
             own_z(r)
         if r < OWN_X:
             own_x(r)
-    for r in range(ROUNDS):
-        own_s(r)
 
     a_copy = []
     for a in range(4):
@@ -399,17 +399,20 @@
         owns = len(OWNS[i])
         osrc, psrc = pl.ds(off[i], owns), pl.ds(off[i] + owns, NP[i])
         pspan, lspan = pl.ds(poff[i], NP[i]), pl.ds(poff[i] - poff[LATE], NP[i])
-        zs[psrc] = total(h_oth, psrc).astype(BF16)
-        xc[i, 2] = cp.go(zs.at[psrc], xr2.at[lspan], pairz)
-        zs[osrc] = total(h_oth, osrc).astype(BF16)
-        zc[i] = cp.go(zs.at[osrc], zr.at[osrc], zlp)
-        xs[pspan] = total(h_own, psrc).astype(BF16)
-        xc[i] = cp.go(xs.at[pspan], xr.at[pspan], pair)
-        sown[osrc] = total(h_own, osrc)
+        if NP[i]:
+            zs[psrc] = total(h_oth, psrc).astype(BF16)
+            xc[i, 2] = cp.go(zs.at[psrc], xr2.at[lspan], pairz)
+            xs[pspan] = total(h_own, psrc).astype(BF16)
+            xc[i] = cp.go(xs.at[pspan], xr.at[pspan], pair)
+        if owns:
+            zs[osrc] = total(h_oth, osrc).astype(BF16)
+            zc[i] = cp.go(zs.at[osrc], zr.at[osrc], zlp)
+            sown[osrc] = total(h_own, osrc)
 
     def c4(i):
         owns = len(OWNS[i])
-        zc[i].wait_recv()
+        if owns or i < LATE:
+            zc[i].wait_recv()
         if NP[i] and i < LATE:
             src = pl.ds(off[i] + owns, NP[i])
             span = pl.ds(poff[i], NP[i])
@@ -423,7 +426,7 @@
     def c5(i):
         if NP[i]:
             xc[i].wait_recv()
-        if i >= LATE:
+        if i >= LATE and NP[i]:
             xc[i, 2].wait_recv()
         for n, (_, r, a) in enumerate(PAIRS[i]):
             done = xr[poff[i] + n]
@@ -438,14 +441,23 @@
         "c1": c1, "c2": c2, "c3": c3, "c4": c4, "c5": c5,
         "l3": l3, "l4": l4, "l5": l5, "l6": l6, "l7": l7, "l8": l8, "l9": l9, "la": la, "l2": l2,
     }
+    old = [0, 0]
+
+    def settle():
+        for copy in cp.sent[old[0] : old[1]]:
+            copy.wait_send()
+        old[0], old[1] = old[1], len(cp.sent)
+
     for step in STEPS:
-        if step[0] == "l":
+        if step == "f":
+            settle()
+        elif step[0] == "l":
             table[step]()
         else:
             table[step[:2]](int(step[2:]))
     for copy in lc["out"]:
         copy.wait_recv()
-    for copy in cp.sent:
+    for copy in cp.sent[old[0] :]:
         copy.wait_send()
 
 
@@ -494,7 +506,7 @@
             pltpu.VMEM((RANK, KDIM), BF16),
             pltpu.VMEM((512, KDIM), BF16),
             pltpu.VMEM((512, KDIM), BF16),
-            pltpu.VMEM((ROUNDS, 4, 4, ROWS, KDIM), BF16),
+            pltpu.VMEM((ROUNDS, 4, 2, 2, ROWS, KDIM), BF16),
         ]
         + [pltpu.VMEM((4, 2, tiles, SUB, 128), BF16)]
         + [

time: 96.2 us -> 89.7 us (0.932)
  Pallas kernels: 95.4 us -> 88.5 us
    pallas_call x1, Pallas kernels: 93.1 us -> 86.3 us  [body(): pl.pallas_call(kernel, out_shape=(jax.ShapeDtypeStruct((2, 2, ROUNDS, ROW...]
where the time goes in v3:
time: 89.7 us; the launch traced here: 89.2 us
  Pallas kernels  88.5 us (99%)
    pallas_call x1, Pallas kernels, body(): pl.pallas_call(kernel, out_shape=(jax.ShapeDtypeStruct((2, 2, ROUNDS, ROW...  86.3 us
    pallas_call x1, Pallas kernels, body(): pl.pallas_call(finish, out_shape=(jax.ShapeDtypeStruct((TOK, 512), BF16),...  2.29 us

profile of v3, /device:TPU:1, one launch (start us, length us, event | category | flops | bytes accessed | tf_op | source)
XLA Modules:
  0.0 89.2 jit_solution(14317102958266153286)
XLA Ops:
  0.6 86.3 %shard_map.94 = (bf16[2,2,8,16,512]{4,3,2,1,0:T(8,128)(2,1)}, f32[4,2,8,512]{3,2,1,0:T(8,128)}, bf16[2,4,4,16,128]{4,3,2,1,0:T(8,128)(2,1)}, bf16[2,128,128]{2,1,0:T(8,128)(2,1)}) custom-call(bf16[512,512]{1,0:T(8,128)(2,1)} %x_in.1, bf16[512,1792]{1,0:T(8,128)(2,1)} %gate_in.1, bf16[512,1792]{1,0:T(8,128)(2,1)} %hid_in.1, bf16[128,1792]{1,0:T(8,128)(2,1)} %w_in.1, ...), custom_call_target="tpu_custom_call" | custom-call | tf_op jit(solution)/shard_map/pallas_call | solution.py:491
  86.9 2.3 %shard_map.95 = (bf16[512,512]{1,0:T(8,128)(2,1)}, f32[4,4096]{1,0:T(4,128)}, f32[128,512]{1,0:T(8,128)}) custom-call(bf16[512,512]{1,0:T(8,128)(2,1)} %bitcast.4, f32[4,2,8,512]{3,2,1,0:T(8,128)} %get-tuple-element.8.feat_ref, bf16[2,4,4,16,128]{4,3,2,1,0:T(8,128)(2,1)} %get-tuple-element.9.gcol, bf16[2,128,128]{2,1,0:T(8,128)(2,1)} %get-tuple-element.10.rowb), custom_call_target="tpu_custom_call" | custom-call | tf_op jit(solution)/shard_map/pallas_call | solution.py:538
